TPU v7x, 32 devices: a whole 2x2x4 slice. The times are simulated.
32 devices in a mesh: group: 2 (over y), dp: 4 (over x, core), mp: 4 (over z).
Axes of the slice: x: 2, y: 2, z: 4, core: 2. Of those that a mesh axis runs over, the one named last changes fastest.
Arguments:
- values: bfloat16 [8, 4, 128, 4096], P(('group', 'dp'), 'mp'), parts along dimension 0, may hold values from -0.25 to 0.25
- rows: int32 [8, 4, 128], P(('group', 'dp'), 'mp'), parts along dimension 0, may hold values from 0 to 31, as said below
- cols: int32 [8, 4, 128], P(('group', 'dp'), 'mp'), parts along dimension 0, may hold values from 0 to 31
- counts: int32 [8, 4], P(('group', 'dp'), 'mp'), parts along dimension 0, may hold values from 32 to 128, as said below
- weights: float32 [16384], P(('group', 'dp')), parts along dimension 0, may hold values from 0.2 to 5
- probes: bfloat16 [256, 64, 64], P(('group', 'mp'), 'dp'), parts along dimension 0, may hold values from -6 to 6
Outputs:
- sketch: float32 [256, 64, 64], P(('group', 'mp'), 'dp'), parts along dimension 0
There are 2 independent parts, one for each index of `group`. A program takes and returns all parts, laid end to end along the dimension named above; each array names one. Nothing has to cross between parts.
Inputs may be any that keep to these rules, and one draw needn't show every extreme that they name: Within one device the pairs (rows, cols) of its 128 slots are all distinct. `counts`: the live slots of a device are its first ones; some device has all 128 live.
All inputs are finite; a program needn't handle non-finite values.
Results may differ from a plain program's by a relative error of at most 0.0023.
Values may be sent and summed in bfloat16 or wider, within the bound.
A program may use at most 64 MiB of HBM per device.

v0:
```python
import jax
import jax.numpy as jnp
from jax import lax
from jax.sharding import PartitionSpec as P

BS = 64


def body(values, rows, cols, counts, weights, probes):
    side = BS
    slots = values.shape[2]
    blocks = values[0, 0].reshape(slots, side, side)
    row_ids = rows[0, 0]
    col_ids = cols[0, 0]
    cell_blocks = probes.shape[0]
    data_blocks = weights.shape[0] // side
    live = jnp.arange(slots, dtype=jnp.int32) < counts[0, 0]
    masked = jnp.where(live[:, None, None], blocks, jnp.zeros_like(blocks))
    gathered = lax.all_gather(probes, "dp", axis=1, tiled=True)
    chosen_panel = jnp.take(gathered, col_ids, axis=0)
    products = jnp.einsum("bij,bjp->bip", masked, chosen_panel, preferred_element_type=jnp.float32)
    local_pred = jax.ops.segment_sum(products, row_ids, num_segments=data_blocks)
    predicted = lax.psum(local_pred, "mp")
    weighted = (weights.reshape(data_blocks, side, 1) * predicted).astype(jnp.bfloat16)
    chosen_rows = jnp.take(weighted, row_ids, axis=0)
    back = jnp.einsum("bij,bip->bjp", masked, chosen_rows, preferred_element_type=jnp.float32)
    local_sketch = jax.ops.segment_sum(back, col_ids, num_segments=cell_blocks)
    return lax.psum_scatter(local_sketch, "dp", scatter_dimension=1, tiled=True)


def solution(mesh):
    placed = (
        P(("group", "dp"), "mp", None, None),
        P(("group", "dp"), "mp", None),
        P(("group", "dp"), "mp", None),
        P(("group", "dp"), "mp"),
        P(("group", "dp")),
        P(("group", "mp"), "dp", None),
    )
    return jax.shard_map(
        body, mesh=mesh, in_specs=placed, out_specs=P(("group", "mp"), "dp", None), check_vma=False
    )
```

profile of v0, /device:TPU:0, one launch (start us, length us, event | category | flops | bytes accessed | tf_op | source)
XLA Modules:
  0.0 150.5 jit_solution(2329479139108610776)
XLA Ops:
  6.5 0.0 all-reduce.2.cloned.1.call-start
  6.5 0.7 compare_select_fusion.1
  7.2 0.7 compare_and_fusion.1
  7.9 1.6 %copy.8 = bf16[1,1,128,4096]{2,3,1,0:T(8,128)(2,1)S(1)} copy(bf16[1,1,128,4096]{3,2,1,0:T(8,128)(2,1)} %param.8) | data formatting | bytes 2097152 | tf_op args[0]
  10.1 0.1 broadcast_select_fusion
  10.2 0.0 copy-start.2
  10.2 3.5 %copy.9 = bf16[128,64,64]{1,2,0:T(8,128)(2,1)S(1)} copy(bf16[128,64,64]{0,2,1:T(8,128)(2,1)S(1)} %broadcast_select_fusion) | data formatting | bytes 2097152 | tf_op jit(solution)/shard_map/jit(_where)/select_n | solution.py:18
  13.7 0.0 copy-done.2
  13.7 8.6 %all_gather.3 = bf16[32,64,64]{2,1,0:T(8,128)(2,1)S(1)} all-gather(bf16[32,16,64]{2,1,0:T(8,128)(2,1)S(1)} %copy-done.2), channel_id=1, replica_groups=mesh['group'=2,'dp'=4,'mp'=4] {'dp'}, dimensions={1}, use_global_device_ids=true | all-gather | bytes 327680 | tf_op jit(solution)/shard_map/all_gather | solution.py:19
  22.4 2.1 %gather_fusion = bf16[128,64,64]{2,1,0:T(8,128)(2,1)} fusion(bf16[32,64,64]{2,1,0:T(8,128)(2,1)S(1)} %all_gather.3, s32[1024]{0:T(1024)S(1)} %pad_clamp_fusion.1), kind=kCustom, calls=%fused_computation.clone | custom fusion | bytes 2097664 | tf_op jit(solution)/shard_map/jit(_take)/gather | solution.py:20
  24.5 0.0 copy-start.4
  24.5 4.5 %fusion.2 = f32[128,64,64]{2,1,0:T(8,128)} fusion(bf16[128,64,64]{1,2,0:T(8,128)(2,1)S(1)} %copy.9, bf16[128,64,64]{2,1,0:T(8,128)(2,1)} %gather_fusion, pred[128]{0:T(512)(128)(4,1)S(1)} %compare_and_fusion.1), kind=kOutput, calls=%fused_computation.6 | convolution fusion | flops 67633152 | bytes 4194432 | tf_op jit(solution)/shard_map/bij,bjp->bip/dot_general | solution.py:21
  29.1 0.1 broadcast.10.clone
  29.2 0.0 copy-done.4
  29.2 0.0 copy-start.3
  29.2 13.5 %scatter_fusion = f32[32,64,64]{2,1,0:T(8,128)S(1)} fusion(f32[32,64,64]{2,1,0:T(8,128)S(1)} %broadcast.10.clone, s32[128]{0:T(128)S(1)} %bitcast.14, f32[128,64,64]{2,1,0:T(8,128)} %fusion.2), kind=kCustom, calls=%fused_computation.2 | custom fusion | flops 524288 | bytes 6291968 | tf_op jit(solution)/shard_map/scatter-add | solution.py:22
  42.7 0.0 copy-start.1
  42.7 1.0 copy-done.1
  43.7 0.0 all-reduce.2.cloned.1.call-update
  43.7 0.0 reduce-scatter.2.cloned.1.call-start
  43.8 0.0 copy-done.3
  43.8 0.1 mul.10
  43.9 52.7 %all-reduce.2.cloned.1.call-done = f32[32,64,64]{2,1,0:T(8,128)} async-done(((f32[32,64,64]{2,1,0:T(8,128)}), f32[32,64,64]{2,1,0:T(8,128)}) %all-reduce.2.cloned.1.call-update) | async-done | bytes 524304 | tf_op jit(solution)/shard_map/psum | solution.py:23
  96.6 1.6 %multiply_convert_fusion = bf16[32,64,64]{2,1,0:T(8,128)(2,1)S(1)} fusion(f32[32,64,64]{2,1,0:T(8,128)} %all-reduce.2.cloned.1.call-done, f32[32,64]{1,0:T(8,128)S(1)} %mul.10), kind=kLoop, calls=%fused_computation.12 | loop fusion | flops 262144 | bytes 794624 | tf_op jit(solution)/shard_map/convert_element_type | solution.py:24
  98.1 2.1 %gather_fusion.1 = bf16[128,64,64]{2,1,0:T(8,128)(2,1)} fusion(bf16[32,64,64]{2,1,0:T(8,128)(2,1)S(1)} %multiply_convert_fusion, s32[1024]{0:T(1024)S(1)} %pad_clamp_fusion), kind=kCustom, calls=%fused_computation.1.clone | custom fusion | bytes 2097664 | tf_op jit(solution)/shard_map/jit(_take)/gather | solution.py:25
  100.3 0.0 copy-start.5
  100.3 4.3 %fusion = f32[128,64,64]{2,1,0:T(8,128)} fusion(bf16[128,64,64]{1,2,0:T(8,128)(2,1)S(1)} %copy.9, bf16[128,64,64]{2,1,0:T(8,128)(2,1)} %gather_fusion.1, pred[128]{0:T(512)(128)(4,1)S(1)} %compare_and_fusion), kind=kOutput, calls=%fused_computation.4 | convolution fusion | flops 67633152 | bytes 4194432 | tf_op jit(solution)/shard_map/bij,bip->bjp/dot_general | solution.py:26
  104.6 0.1 broadcast.10
  104.7 0.0 copy-done.5
  104.7 13.5 %scatter_fusion.1 = f32[32,64,64]{2,1,0:T(8,128)S(1)} fusion(f32[32,64,64]{2,1,0:T(8,128)S(1)} %broadcast.10, s32[128]{0:T(128)S(1)} %bitcast.15, f32[128,64,64]{2,1,0:T(8,128)} %fusion), kind=kCustom, calls=%fused_computation.3 | custom fusion | flops 524288 | bytes 6291968 | tf_op jit(solution)/shard_map/scatter-add | solution.py:27
  118.2 0.0 copy-start
  118.2 1.0 copy-done
  119.2 0.0 reduce-scatter.2.cloned.1.call-update
  119.2 24.4 %reduce-scatter.2.cloned.1.call-done = f32[32,16,64]{2,1,0:T(8,128)} async-done(((f32[32,64,64]{2,1,0:T(8,128)}), f32[32,16,64]{2,1,0:T(8,128)}) %reduce-scatter.2.cloned.1.call-update) | async-done | bytes 131088 | tf_op jit(solution)/shard_map/reduce_scatter | solution.py:28
  (5 shorter events, 0.0 us)
Async XLA Ops:
  6.5 90.0 %all-reduce.2.cloned.1.call-start = ((), (), s32[]{:S(2)}) async-start(), calls=%async_computation.1 | async-start | bytes 2097152 | tf_op jit(solution)/shard_map/psum | solution.py:23
  10.2 3.5 %copy-start.2 = (bf16[32,16,64]{2,1,0:T(8,128)(2,1)S(1)}, bf16[32,16,64]{2,1,0:T(8,128)(2,1)}, u32[]{:S(2)}) copy-start(bf16[32,16,64]{2,1,0:T(8,128)(2,1)} %param.13) | copy-start | bytes 196612
  24.5 4.7 %copy-start.4 = (s32[1,1,128]{2,1,0:T(1,128)S(1)}, s32[1,1,128]{2,1,0:T(1,128)}, u32[]{:S(2)}) copy-start(s32[1,1,128]{2,1,0:T(1,128)} %param.9) | copy-start | bytes 1540
  29.2 14.6 %copy-start.3 = (f32[2048]{0:T(1024)S(1)}, f32[2048]{0:T(1024)}, u32[]{:S(2)}) copy-start(f32[2048]{0:T(1024)} %param.12) | copy-start | bytes 24580
  42.7 1.0 copy-start.1
  43.7 99.9 %reduce-scatter.2.cloned.1.call-start = ((), (), s32[]{:S(2)}) async-start(), calls=%async_computation.2 | async-start | bytes 1310720 | tf_op jit(solution)/shard_map/reduce_scatter | solution.py:28
  100.3 4.4 %copy-start.5 = (s32[1,1,128]{2,1,0:T(1,128)S(1)}, s32[1,1,128]{2,1,0:T(1,128)}, u32[]{:S(2)}) copy-start(s32[1,1,128]{2,1,0:T(1,128)} %param.10) | copy-start | bytes 1540
  118.2 1.0 copy-start
Sparse Core Ops, SparseCore 0:
  43.9 52.6 all-reduce.1
  119.4 24.2 reduce-scatter.1
where the time goes:
time: 152 us; the launch traced here: 150 us
  waiting for transfers between devices  77.1 us (51%)
  other arithmetic  30 us (20%)
  between operations  14.2 us (9%)
  local copies, waits for them, and re-layouts  11.7 us (8%)
  matrix products  8.86 us (6%)
  blocking collectives  8.62 us (6%)
    psum x1, waiting for transfers between devices, body(): predicted = lax.psum(local_pred, 'mp')  52.7 us
    reduce_scatter x1, waiting for transfers between devices, body(): return lax.psum_scatter(local_sketch, 'dp', scatter_dimension=1, tiled=True)  24.4 us
    scatter-add x1, other arithmetic, body(): local_sketch = jax.ops.segment_sum(back, col_ids, num_segments=cell_blocks)  13.5 us
    scatter-add x1, other arithmetic, body(): jax.ops.segment_sum(products, row_ids, num_segments=data_blocks)  13.5 us
    all_gather x1, blocking collectives, body(): gathered = lax.all_gather(probes, 'dp', axis=1, tiled=True)  8.62 us
    dot_general x1, matrix products, body(): jnp.einsum('bij,bjp->bip', masked, chosen_panel, preferred_element_type=j...  4.54 us
    dot_general x1, matrix products, body(): jnp.einsum('bij,bip->bjp', masked, chosen_rows, preferred_element_type=jn...  4.31 us
    unnamed x13, local copies, waits for them, and re-layouts  3.63 us
  transfers between devices with their start and end apart: 2, of which 2 were waited for; matrix products, arithmetic and copies ran while one was open for 0% of the time, Pallas kernels for 0%

commit v1 on v0

v1 whole, which is shorter than its diff:
```python
import functools

import jax
import jax.numpy as jnp
from jax import lax
from jax.experimental import pallas as pl
from jax.experimental.pallas import tpu as pltpu
from jax.sharding import PartitionSpec as P

BS = 64
MESH = pl.DeviceIdType.MESH
BF16 = jnp.bfloat16
F32 = jnp.float32
PRED = jnp.float32


def both_halves(x):
    low, high = x[:, :BS], x[:, BS:]
    return jnp.concatenate([low, low], axis=1), jnp.concatenate([high, high], axis=1)


def kernel(n_dp, n_mp, n_data, n_cells,
           table, fwd_blocks, bwd_blocks, probes, weights, out,
           gathered, wide_f32, wide, fwd, bwd, psend, precv, own_pred, wgather, wide_w,
           ssend, srecv, own_sketch,
           gs, gr, ps, pr, ws, wr, ss, sr):
    dp, mp = lax.axis_index("dp"), lax.axis_index("mp")
    share = BS // n_dp
    owned = n_data // n_mp
    pairs = owned // 2
    half_cells = n_cells // 2
    side = lax.broadcasted_iota(jnp.int32, (BS, 2 * BS), 1) < BS

    barrier = pltpu.get_barrier_semaphore()
    for off in range(1, n_dp):
        pl.semaphore_signal(barrier, inc=1, device_id={"dp": lax.rem(dp + off, n_dp)}, device_id_type=MESH)
    for off in range(1, n_mp):
        pl.semaphore_signal(barrier, inc=1, device_id={"mp": lax.rem(mp + off, n_mp)}, device_id_type=MESH)
    pl.semaphore_wait(barrier, n_dp + n_mp - 2)

    def remote(src, dst, send, recv, axis, peer):
        return pltpu.make_async_remote_copy(
            src_ref=src, dst_ref=dst, send_sem=send, recv_sem=recv,
            device_id={axis: peer}, device_id_type=MESH)

    for off in range(1, n_dp):
        remote(probes, gathered.at[off - 1], gs.at[off - 1], gr.at[off - 1],
               "dp", lax.rem(dp + off, n_dp)).start()

    def build(blocks, strips, count, first, second):
        def one(block, carry):
            base = pl.multiple_of(block * BS, BS)
            for k in range(count // 2):
                a = blocks[table[block * first + (2 * k) * second]]
                b = blocks[table[block * first + (2 * k + 1) * second]]
                strips[pl.ds(base, BS), 2 * k * BS:(2 * k + 2) * BS] = jnp.where(side, a, b)
            return carry
        return one

    lax.fori_loop(0, n_data, build(fwd_blocks, fwd, n_cells, n_cells, 1), 0)

    def place(source, d):
        rows = source.astype(F32)
        start = pl.multiple_of(d * share, share)
        for c in range(half_cells):
            wide_f32[c, pl.ds(start, share), :] = rows[c * share:(c + 1) * share]

    place(probes[...], dp)
    for off in range(1, n_dp):
        remote(probes, gathered.at[off - 1], gs.at[off - 1], gr.at[off - 1], "dp", dp).wait_recv()
        place(gathered[off - 1], lax.rem(dp + n_dp - off, n_dp))
    for c in range(half_cells):
        low, high = both_halves(wide_f32[c])
        wide[c * BS:(c + 1) * BS] = low.astype(BF16)
        wide[(half_cells + c) * BS:(half_cells + c + 1) * BS] = high.astype(BF16)

    half = lax.broadcasted_iota(jnp.int32, (pairs * BS, 2 * BS), 1) < BS

    def predict(peer):
        start = pl.multiple_of(peer * (owned * BS), owned * BS)
        full = jnp.dot(fwd[pl.ds(start, owned * BS), :], wide[...], preferred_element_type=F32)
        return jnp.where(half, full[:pairs * BS], full[pairs * BS:])

    for off in range(1, n_mp):
        peer = lax.rem(mp + off, n_mp)
        psend[off - 1] = predict(peer).astype(PRED)
        remote(psend.at[off - 1], precv.at[off - 1], ps.at[off - 1], pr.at[off - 1], "mp", peer).start()
    own_pred[...] = predict(mp)

    lax.fori_loop(0, n_cells, build(bwd_blocks, bwd, n_data, 1, n_cells), 0)

    total = own_pred[...]
    for off in range(1, n_mp):
        remote(psend.at[off - 1], precv.at[off - 1], ps.at[off - 1], pr.at[off - 1], "mp", mp).wait_recv()
        total = total + precv[off - 1].astype(F32)
    wgather[0] = (weights[...] * total).astype(BF16)
    for off in range(1, n_mp):
        remote(wgather.at[0], wgather.at[off], ws.at[off - 1], wr.at[off - 1],
               "mp", lax.rem(mp + off, n_mp)).start()

    def place_w(source, k):
        low, high = both_halves(source.astype(F32))
        start = pl.multiple_of(k * (owned * BS), pairs * BS)
        wide_w[pl.ds(start, pairs * BS), :] = low.astype(BF16)
        wide_w[pl.ds(start + pairs * BS, pairs * BS), :] = high.astype(BF16)

    place_w(wgather[0], mp)
    for off in range(1, n_mp):
        remote(wgather.at[0], wgather.at[off], ws.at[off - 1], wr.at[off - 1], "mp", mp).wait_recv()
        place_w(wgather[off], lax.rem(mp + n_mp - off, n_mp))

    group = 8
    gp = group // 2
    half_g = lax.broadcasted_iota(jnp.int32, (gp * BS, 2 * BS), 1) < BS
    rows = gp * share
    for g in range(n_cells // group):
        full = jnp.dot(bwd[g * group * BS:(g + 1) * group * BS, :], wide_w[...], preferred_element_type=F32)
        packed = jnp.where(half_g, full[:gp * BS], full[gp * BS:])
        for d in range(n_dp):
            part = jnp.concatenate(
                [packed[p * BS + d * share:p * BS + (d + 1) * share] for p in range(gp)], axis=0)
            ssend[d, g * rows:(g + 1) * rows] = part.astype(BF16)

            @pl.when(dp == d)
            def _():
                own_sketch[g * rows:(g + 1) * rows] = part
        for off in range(1, n_dp):
            peer = lax.rem(dp + off, n_dp)
            remote(ssend.at[peer, pl.ds(g * rows, rows)], srecv.at[off - 1, pl.ds(g * rows, rows)],
                   ss.at[off - 1, g], sr.at[off - 1, g], "dp", peer).start()
    for g in range(n_cells // group):
        acc = own_sketch[g * rows:(g + 1) * rows]
        for off in range(1, n_dp):
            remote(ssend.at[0, pl.ds(g * rows, rows)], srecv.at[off - 1, pl.ds(g * rows, rows)],
                   ss.at[off - 1, g], sr.at[off - 1, g], "dp", dp).wait_recv()
            acc = acc + srecv[off - 1, g * rows:(g + 1) * rows].astype(F32)
        for p in range(gp):
            one = acc[p * share:(p + 1) * share]
            out[g * group + p] = one[:, :BS]
            out[g * group + gp + p] = one[:, BS:]

    for off in range(1, n_dp):
        remote(probes, gathered.at[off - 1], gs.at[off - 1], gr.at[off - 1], "dp", dp).wait_send()
        for g in range(n_cells // group):
            remote(ssend.at[0, pl.ds(g * rows, rows)], srecv.at[off - 1, pl.ds(g * rows, rows)],
                   ss.at[off - 1, g], sr.at[off - 1, g], "dp", dp).wait_send()
    for off in range(1, n_mp):
        remote(psend.at[off - 1], precv.at[off - 1], ps.at[off - 1], pr.at[off - 1], "mp", mp).wait_send()
        remote(wgather.at[0], wgather.at[off], ws.at[off - 1], wr.at[off - 1], "mp", mp).wait_send()


def body(n_dp, n_mp, values, rows, cols, counts, weights, probes):
    slots = values.shape[2]
    blocks = values[0, 0].reshape(slots, BS, BS)
    n_cells = probes.shape[0]
    share = probes.shape[1]
    n_data = weights.shape[0] // BS
    owned = n_data // n_mp
    pairs = owned // 2
    half_cells = n_cells // 2
    groups = n_cells // 8
    srows = 4 * share

    live = jnp.arange(slots, dtype=jnp.int32) < counts[0, 0]
    where = jnp.where(live, rows[0, 0] * n_cells + cols[0, 0], -1)
    places = jnp.arange(n_data * n_cells, dtype=jnp.int32)
    hit = places[:, None] == where[None, :]
    table = jnp.min(jnp.where(hit, jnp.arange(slots, dtype=jnp.int32)[None, :], slots), axis=1)

    blank = jnp.zeros((1, BS, 2 * BS), BF16)
    fwd_blocks = jnp.concatenate([jnp.concatenate([blocks, blocks], axis=2), blank], axis=0)
    turned = blocks.transpose(0, 2, 1)
    bwd_blocks = jnp.concatenate([jnp.concatenate([turned, turned], axis=2), blank], axis=0)
    packed = jnp.concatenate([probes[:half_cells], probes[half_cells:]], axis=2)
    packed = packed.reshape(half_cells * share, 2 * BS)
    mine = lax.dynamic_slice_in_dim(weights, lax.axis_index("mp") * (owned * BS), owned * BS)
    mine = mine.reshape(2, pairs * BS, 1)
    mine = jnp.concatenate(
        [jnp.broadcast_to(mine[0], (pairs * BS, BS)), jnp.broadcast_to(mine[1], (pairs * BS, BS))], axis=1)

    vmem = pl.BlockSpec(memory_space=pltpu.VMEM)
    dma = pltpu.SemaphoreType.DMA
    return pl.pallas_call(
        functools.partial(kernel, n_dp, n_mp, n_data, n_cells),
        out_shape=jax.ShapeDtypeStruct((n_cells, share, BS), F32),
        in_specs=[pl.BlockSpec(memory_space=pltpu.SMEM)] + [vmem] * 4,
        out_specs=vmem,
        scratch_shapes=[
            pltpu.VMEM((n_dp - 1, half_cells * share, 2 * BS), BF16),
            pltpu.VMEM((half_cells, BS, 2 * BS), F32),
            pltpu.VMEM((n_cells * BS, 2 * BS), BF16),
            pltpu.VMEM((n_data * BS, n_cells * BS), BF16),
            pltpu.VMEM((n_cells * BS, n_data * BS), BF16),
            pltpu.VMEM((n_mp - 1, pairs * BS, 2 * BS), PRED),
            pltpu.VMEM((n_mp - 1, pairs * BS, 2 * BS), PRED),
            pltpu.VMEM((pairs * BS, 2 * BS), F32),
            pltpu.VMEM((n_mp, pairs * BS, 2 * BS), BF16),
            pltpu.VMEM((n_data * BS, 2 * BS), BF16),
            pltpu.VMEM((n_dp, groups * srows, 2 * BS), BF16),
            pltpu.VMEM((n_dp - 1, groups * srows, 2 * BS), BF16),
            pltpu.VMEM((groups * srows, 2 * BS), F32),
            dma((n_dp - 1,)), dma((n_dp - 1,)),
            dma((n_mp - 1,)), dma((n_mp - 1,)),
            dma((n_mp - 1,)), dma((n_mp - 1,)),
            dma((n_dp - 1, groups)), dma((n_dp - 1, groups)),
        ],
        compiler_params=pltpu.CompilerParams(
            collective_id=0, has_side_effects=True, vmem_limit_bytes=48 * 1024 * 1024),
    )(table, fwd_blocks, bwd_blocks, packed, mine)


def solution(mesh):
    placed = (
        P(("group", "dp"), "mp", None, None),
        P(("group", "dp"), "mp", None),
        P(("group", "dp"), "mp", None),
        P(("group", "dp"), "mp"),
        P(("group", "dp")),
        P(("group", "mp"), "dp", None),
    )
    return jax.shard_map(
        functools.partial(body, mesh.shape["dp"], mesh.shape["mp"]),
        mesh=mesh, in_specs=placed, out_specs=P(("group", "mp"), "dp", None), check_vma=False
    )
```

time: 152 us -> 58.9 us (0.39)
  waiting for transfers between devices: 77.1 us -> 0 us
  Pallas kernels: 0 us -> 37.9 us
  other arithmetic: 30 us -> 6.95 us
  between operations: 14.2 us -> 0.72 us
  matrix products: 8.86 us -> 0 us
  blocking collectives: 8.62 us -> 0 us
    psum x1 -> x0, waiting for transfers between devices: 52.7 us -> none  [body(): predicted = lax.psum(local_pred, 'mp')]
    pallas_call x0 -> x1, Pallas kernels: none -> 37.9 us  [body(): pl.pallas_call(functools.partial(kernel, n_dp, n_mp, n_data, n_cells), ou...]
    scatter-add x2 -> x0, other arithmetic: 27 us -> none  [the longest x1 13.5 us: body(): local_sketch = jax.ops.segment_sum(back, col_ids, num_segments=cell_blocks)]
    reduce_scatter x1 -> x0, waiting for transfers between devices: 24.4 us -> none  [body(): return lax.psum_scatter(local_sketch, 'dp', scatter_dimension=1, tiled=True)]
    dot_general x2 -> x0, matrix products: 8.86 us -> none  [the longest x1 4.54 us: body(): jnp.einsum('bij,bjp->bip', masked, chosen_panel, preferred_element_type=j...]
    all_gather x1 -> x0, blocking collectives: 8.62 us -> none  [body(): gathered = lax.all_gather(probes, 'dp', axis=1, tiled=True)]
    another operation x2, local copies, waits for them, and re-layouts: 0.21 us -> 8.25 us  [body(): blocks = values[0, 0].reshape(slots, BS, BS)]
    concatenate x0 -> x3, other arithmetic: none -> 6.06 us  [the longest x1 5.86 us: body(): jnp.concatenate([blocks, blocks], axis=2)]
  transfers between devices with their start and end apart: 2 -> 0, of which waited for: 2 -> 0; matrix products, arithmetic and copies ran while one was open for 0% -> 0% of each run, Pallas kernels for 0% -> 0%
where the time goes in v1:
time: 58.9 us; the launch traced here: 58.7 us
  Pallas kernels  37.9 us (64%)
  local copies, waits for them, and re-layouts  13.2 us (22%)
  other arithmetic  6.95 us (12%)
  between operations  0.72 us (1%)
    pallas_call x1, Pallas kernels, body(): pl.pallas_call(functools.partial(kernel, n_dp, n_mp, n_data, n_cells), ou...  37.9 us
    another operation x2, local copies, waits for them, and re-layouts, body(): blocks = values[0, 0].reshape(slots, BS, BS)  8.25 us
    concatenate x1, other arithmetic, body(): jnp.concatenate([blocks, blocks], axis=2)  5.86 us
    unnamed x6, local copies, waits for them, and re-layouts  3.95 us

profile of v1, /device:TPU:0, one launch (start us, length us, event | category | flops | bytes accessed | tf_op | source)
XLA Modules:
  0.0 58.7 jit_solution(13560477689687051627)
XLA Ops:
  0.7 0.7 %compare_select_fusion = s32[128]{0:T(128)S(1)} fusion(s32[1,1,128]{2,1,0:T(1,128)} %param.8, s32[1,1,128]{2,1,0:T(1,128)} %param.7, s32[]{:T(128)} %bitcast.6), kind=kLoop, calls=%fused_computation.11 | loop fusion | flops 512 | bytes 1540 | tf_op jit(solution)/shard_map/jit(_where)/select_n | solution.py:165
  1.3 0.2 select_reduce_fusion.table
  1.5 1.6 %copy.12 = bf16[1,1,128,4096]{2,3,1,0:T(8,128)(2,1)S(1)} copy(bf16[1,1,128,4096]{3,2,1,0:T(8,128)(2,1)} %param.6) | data formatting | bytes 2097152 | tf_op args[0]
  3.2 3.8 %copy.13 = bf16[128,64,64]{2,1,0:T(8,128)(2,1)} copy(bf16[128,64,64]{0,2,1:T(8,128)(2,1)S(1)} %bitcast.8) | data formatting | bytes 2097152 | tf_op jit(solution)/shard_map/reshape;squeeze | solution.py:154
  7.0 4.5 %copy.15 = bf16[128,64,64]{1,2,0:T(8,128)(2,1)} copy(bf16[128,64,64]{0,2,1:T(8,128)(2,1)S(1)} %bitcast.9) | data formatting | bytes 2097152 | tf_op jit(solution)/shard_map/reshape;squeeze | solution.py:154
  11.5 0.0 copy-start.1
  11.5 5.9 %fusion.4 = (bf16[129,64,128]{2,1,0:T(8,128)(2,1)S(1)}, bf16[129,64,128]{2,1,0:T(8,128)(2,1)}) fusion(bf16[128,64,64]{2,1,0:T(8,128)(2,1)} %copy.13, bf16[128,64,64]{2,1,0:T(8,128)(2,1)} %bitcast.10), kind=kLoop, calls=%fused_computation.5 | loop fusion | flops 13737984 | bytes 6324224 | tf_op jit(solution)/shard_map/concatenate | solution.py:171
  17.3 0.0 copy-done.1
  17.3 0.1 pad_maximum_fusion.1
  17.4 0.8 %dynamic_slice.3 = f32[512]{0:T(512)S(1)} dynamic-slice(f32[2048]{0:T(1024)} %param.10, s32[]{:T(128)S(6)} %select_n.17), dynamic_slice_sizes={512} | dynamic-slice | bytes 4100 | tf_op jit(solution)/shard_map/dynamic_slice | solution.py:176
  18.2 0.1 broadcast_in_dim.34
  18.3 0.1 broadcast_in_dim.33
  18.4 0.1 pad_maximum_fusion.weights
  18.5 0.0 copy-start
  18.5 1.6 %copy-done = bf16[129,64,128]{2,1,0:T(8,128)(2,1)S(1)} copy-done((bf16[129,64,128]{2,1,0:T(8,128)(2,1)S(1)}, bf16[129,64,128]{2,1,0:T(8,128)(2,1)}, u32[]{:S(2)}) %copy-start) | copy-done | bytes 2113560
  20.1 37.9 %shard_map.64 = f32[32,16,64]{2,1,0:T(8,128)S(1)} custom-call(s32[1024]{0:T(1024)S(1)} %select_reduce_fusion.table, bf16[129,64,128]{2,1,0:T(8,128)(2,1)S(1)} %get-tuple-element.9.fwd_blocks, bf16[129,64,128]{2,1,0:T(8,128)(2,1)S(1)} %copy-done, bf16[256,128]{1,0:T(8,128)(2,1)S(1)} %bitcast.7, f32[256,128]{1,0:T(8,128)S(1)} %pad_maximum_fusion.weights), custom_call_target="tpu_custom_call" | custom-call | tf_op jit(solution)/shard_map/pallas_call | solution.py:183
  58.0 0.7 %copy.18 = f32[32,16,64]{2,1,0:T(8,128)} copy(f32[32,16,64]{2,1,0:T(8,128)S(1)} %shard_map.64) | data formatting | bytes 262144
  (2 shorter events, 0.0 us)
Async XLA Ops:
  11.5 5.9 %copy-start.1 = (bf16[32,16,64]{2,1,0:T(8,128)(2,1)S(1)}, bf16[32,16,64]{2,1,0:T(8,128)(2,1)}, u32[]{:S(2)}) copy-start(bf16[32,16,64]{2,1,0:T(8,128)(2,1)} %param.11) | copy-start | bytes 196612
  18.5 1.6 %copy-start = (bf16[129,64,128]{2,1,0:T(8,128)(2,1)S(1)}, bf16[129,64,128]{2,1,0:T(8,128)(2,1)}, u32[]{:S(2)}) copy-start(bf16[129,64,128]{2,1,0:T(8,128)(2,1)} %get-tuple-element.10.bwd_blocks) | copy-start | bytes 6340612

commit v2 on v1

v2 whole, which is shorter than its diff:
```python
import functools

import jax
import jax.numpy as jnp
from jax import lax
from jax.experimental import pallas as pl
from jax.experimental.pallas import tpu as pltpu
from jax.sharding import PartitionSpec as P

BS = 64
MESH = pl.DeviceIdType.MESH
BF16 = jnp.bfloat16
F32 = jnp.float32


def both_halves(x):
    low, high = x[:, :BS], x[:, BS:]
    return jnp.concatenate([low, low], axis=1), jnp.concatenate([high, high], axis=1)


def kernel(n_dp, n_mp, n_data, n_cells, slots,
           table, values, probes, weights, out,
           flat, plain, turned, packed, gathered, wide_f32, wide, strips, psend, precv, own_pred,
           wgather, total_back, ssend, srecv, own_sketch,
           gs, gr, ps, pr, ws, wr, ss, sr):
    dp, mp = lax.axis_index("dp"), lax.axis_index("mp")
    share = BS // n_dp
    owned = n_data // n_mp
    pairs = owned // 2
    depth = owned * BS
    half_cells = n_cells // 2
    hb = BS // 2
    side = lax.broadcasted_iota(jnp.int32, (hb, 2 * BS), 1) < BS

    barrier = pltpu.get_barrier_semaphore()
    for off in range(1, n_dp):
        pl.semaphore_signal(barrier, inc=1, device_id={"dp": lax.rem(dp + off, n_dp)}, device_id_type=MESH)
    for off in range(1, n_mp):
        pl.semaphore_signal(barrier, inc=1, device_id={"mp": lax.rem(mp + off, n_mp)}, device_id_type=MESH)

    for c in range(half_cells):
        flat[c * share:(c + 1) * share] = jnp.concatenate([probes[c], probes[half_cells + c]], axis=1).astype(F32)
    packed[...] = flat[0:half_cells * share].astype(BF16)
    pl.semaphore_wait(barrier, n_dp + n_mp - 2)

    def remote(src, dst, send, recv, axis, peer):
        return pltpu.make_async_remote_copy(
            src_ref=src, dst_ref=dst, send_sem=send, recv_sem=recv,
            device_id={axis: peer}, device_id_type=MESH)

    for off in range(1, n_dp):
        remote(packed, gathered.at[off - 1], gs.at[off - 1], gr.at[off - 1],
               "dp", lax.rem(dp + off, n_dp)).start()

    for q in range(hb):
        flat[pl.ds(q, slots, stride=hb), :] = values[:, q * 2 * BS:(q + 1) * 2 * BS].astype(F32)

    def turn(s, carry):
        start = pl.multiple_of(s * (8 * hb), 8 * hb)
        rows = flat[pl.ds(start, 8 * hb), :]
        plain[pl.ds(s * 8, 8)] = rows.astype(BF16).reshape(8, hb, 2 * BS)
        turned[pl.ds(s * 8, 8)] = pltpu.roll(rows, BS, 1).astype(BF16).reshape(8, hb, 2 * BS)
        return carry

    lax.fori_loop(0, slots // 8, turn, 0)
    plain[slots] = jnp.zeros((hb, 2 * BS), BF16)
    turned[slots] = jnp.zeros((hb, 2 * BS), BF16)

    def build(block, carry):
        base = pl.multiple_of(block * BS, BS)
        for k in range(n_cells // 2):
            a = table[block * n_cells + 2 * k]
            b = table[block * n_cells + 2 * k + 1]
            lanes = slice(2 * k * BS, (2 * k + 2) * BS)
            strips[pl.ds(base, hb), lanes] = jnp.where(side, plain[a], turned[b])
            strips[pl.ds(base + hb, hb), lanes] = jnp.where(side, turned[a], plain[b])
        return carry

    lax.fori_loop(0, n_data, build, 0)

    def place(source, d):
        rows = source.astype(F32)
        start = pl.multiple_of(d * share, share)
        for c in range(half_cells):
            wide_f32[c, pl.ds(start, share), :] = rows[c * share:(c + 1) * share]

    place(packed[...], dp)
    for off in range(1, n_dp):
        remote(packed, gathered.at[off - 1], gs.at[off - 1], gr.at[off - 1], "dp", dp).wait_recv()
        place(gathered[off - 1], lax.rem(dp + n_dp - off, n_dp))
    for c in range(half_cells):
        low, high = both_halves(wide_f32[c])
        wide[c * BS:(c + 1) * BS] = low.astype(BF16)
        wide[(half_cells + c) * BS:(half_cells + c + 1) * BS] = high.astype(BF16)

    half = lax.broadcasted_iota(jnp.int32, (pairs * BS, 2 * BS), 1) < BS

    def rows_of(k):
        return pl.ds(pl.multiple_of(k * depth, depth), depth)

    def predict(peer):
        full = jnp.dot(strips[rows_of(peer), :], wide[...], preferred_element_type=F32)
        return jnp.where(half, full[:pairs * BS], full[pairs * BS:])

    for off in range(1, n_mp):
        peer = lax.rem(mp + off, n_mp)
        psend[off - 1] = predict(peer)
        remote(psend.at[off - 1], precv.at[off - 1], ps.at[off - 1], pr.at[off - 1], "mp", peer).start()
    own_pred[...] = predict(mp)

    i0 = lax.broadcasted_iota(jnp.int32, (2 * BS, 2 * BS), 0)
    i1 = lax.broadcasted_iota(jnp.int32, (2 * BS, 2 * BS), 1)
    inner = lax.rem(i1, BS)
    origin = i1 - inner + 2 * lax.rem(inner, hb) + inner // hb
    order = (i0 == origin).astype(F32)
    mine = weights[:, pl.ds(pl.multiple_of(mp * depth, depth), depth)]
    sorted_w = jnp.concatenate(
        [jnp.dot(jnp.broadcast_to(mine[:, k * 2 * BS:(k + 1) * 2 * BS], (8, 2 * BS)), order,
                 precision=lax.Precision.HIGHEST, preferred_element_type=F32) for k in range(owned // 2)], axis=1)
    factor = jnp.concatenate(
        [jnp.broadcast_to(sorted_w[0:1, :pairs * BS], (BS, pairs * BS)),
         jnp.broadcast_to(sorted_w[0:1, pairs * BS:], (BS, pairs * BS))], axis=0)

    total = own_pred[...]
    for off in range(1, n_mp):
        remote(psend.at[off - 1], precv.at[off - 1], ps.at[off - 1], pr.at[off - 1], "mp", mp).wait_recv()
        total = total + precv[off - 1]
    wgather[0] = (factor * total.T).astype(BF16)
    for off in range(1, n_mp):
        remote(wgather.at[0], wgather.at[off], ws.at[off - 1], wr.at[off - 1],
               "mp", lax.rem(mp + off, n_mp)).start()

    group = 8
    gp = group // 2
    cols = group * BS
    rows = gp * share

    def part_of(slot, k, g):
        chunk = wgather[slot]
        left = jnp.concatenate([chunk[:BS], chunk[BS:]], axis=1)
        return jnp.dot(left, strips[rows_of(k), g * cols:(g + 1) * cols], preferred_element_type=F32)

    n_groups = n_cells // group
    for off in range(n_mp):
        if off:
            remote(wgather.at[0], wgather.at[off], ws.at[off - 1], wr.at[off - 1], "mp", mp).wait_recv()
        for g in range(n_groups):
            lanes = slice(g * cols, (g + 1) * cols)
            part = part_of(off, lax.rem(mp + n_mp - off, n_mp), g)
            if off:
                part = part + total_back[:, lanes]
            if off < n_mp - 1:
                total_back[:, lanes] = part
                continue
            both = jnp.concatenate([part[:, :gp * BS], part[:, gp * BS:]], axis=0).T
            for d in range(n_dp):
                piece = jnp.concatenate(
                    [both[p * BS + d * share:p * BS + (d + 1) * share] for p in range(gp)], axis=0)
                ssend[d, g * rows:(g + 1) * rows] = piece.astype(BF16)

                @pl.when(dp == d)
                def _():
                    own_sketch[g * rows:(g + 1) * rows] = piece
            for o in range(1, n_dp):
                peer = lax.rem(dp + o, n_dp)
                remote(ssend.at[peer, pl.ds(g * rows, rows)], srecv.at[o - 1, pl.ds(g * rows, rows)],
                       ss.at[o - 1, g], sr.at[o - 1, g], "dp", peer).start()

    for g in range(n_groups):
        acc = own_sketch[g * rows:(g + 1) * rows]
        for off in range(1, n_dp):
            remote(ssend.at[0, pl.ds(g * rows, rows)], srecv.at[off - 1, pl.ds(g * rows, rows)],
                   ss.at[off - 1, g], sr.at[off - 1, g], "dp", dp).wait_recv()
            acc = acc + srecv[off - 1, g * rows:(g + 1) * rows].astype(F32)
        for p in range(gp):
            one = acc[p * share:(p + 1) * share]
            out[g * group + p] = one[:, :BS]
            out[g * group + gp + p] = one[:, BS:]

    for off in range(1, n_dp):
        remote(packed, gathered.at[off - 1], gs.at[off - 1], gr.at[off - 1], "dp", dp).wait_send()
        for g in range(n_groups):
            remote(ssend.at[0, pl.ds(g * rows, rows)], srecv.at[off - 1, pl.ds(g * rows, rows)],
                   ss.at[off - 1, g], sr.at[off - 1, g], "dp", dp).wait_send()
    for off in range(1, n_mp):
        remote(psend.at[off - 1], precv.at[off - 1], ps.at[off - 1], pr.at[off - 1], "mp", mp).wait_send()
        remote(wgather.at[0], wgather.at[off], ws.at[off - 1], wr.at[off - 1], "mp", mp).wait_send()


def body(n_dp, n_mp, values, rows, cols, counts, weights, probes):
    slots = values.shape[2]
    n_cells = probes.shape[0]
    share = probes.shape[1]
    n_data = weights.shape[0] // BS
    owned = n_data // n_mp
    pairs = owned // 2
    half_cells = n_cells // 2
    groups = n_cells // 8
    srows = 4 * share

    live = jnp.arange(slots, dtype=jnp.int32) < counts[0, 0]
    where = jnp.where(live, rows[0, 0] * n_cells + cols[0, 0], -1)
    places = jnp.arange(n_data * n_cells, dtype=jnp.int32)
    hit = places[:, None] == where[None, :]
    table = jnp.min(jnp.where(hit, jnp.arange(slots, dtype=jnp.int32)[None, :], slots), axis=1)

    vmem = pl.BlockSpec(memory_space=pltpu.VMEM)
    dma = pltpu.SemaphoreType.DMA
    return pl.pallas_call(
        functools.partial(kernel, n_dp, n_mp, n_data, n_cells, slots),
        out_shape=jax.ShapeDtypeStruct((n_cells, share, BS), F32),
        in_specs=[pl.BlockSpec(memory_space=pltpu.SMEM)] + [vmem] * 3,
        out_specs=vmem,
        scratch_shapes=[
            pltpu.VMEM((slots * BS // 2, 2 * BS), F32),
            pltpu.VMEM((slots + 1, BS // 2, 2 * BS), BF16),
            pltpu.VMEM((slots + 1, BS // 2, 2 * BS), BF16),
            pltpu.VMEM((half_cells * share, 2 * BS), BF16),
            pltpu.VMEM((n_dp - 1, half_cells * share, 2 * BS), BF16),
            pltpu.VMEM((half_cells, BS, 2 * BS), F32),
            pltpu.VMEM((n_cells * BS, 2 * BS), BF16),
            pltpu.VMEM((n_data * BS, n_cells * BS), BF16),
            pltpu.VMEM((n_mp - 1, pairs * BS, 2 * BS), F32),
            pltpu.VMEM((n_mp - 1, pairs * BS, 2 * BS), F32),
            pltpu.VMEM((pairs * BS, 2 * BS), F32),
            pltpu.VMEM((n_mp, 2 * BS, pairs * BS), BF16),
            pltpu.VMEM((BS, n_cells * BS), F32),
            pltpu.VMEM((n_dp, groups * srows, 2 * BS), BF16),
            pltpu.VMEM((n_dp - 1, groups * srows, 2 * BS), BF16),
            pltpu.VMEM((groups * srows, 2 * BS), F32),
            dma((n_dp - 1,)), dma((n_dp - 1,)),
            dma((n_mp - 1,)), dma((n_mp - 1,)),
            dma((n_mp - 1,)), dma((n_mp - 1,)),
            dma((n_dp - 1, groups)), dma((n_dp - 1, groups)),
        ],
        compiler_params=pltpu.CompilerParams(
            collective_id=0, has_side_effects=True, vmem_limit_bytes=48 * 1024 * 1024),
    )(table, values[0, 0], probes, weights.reshape(1, -1))


def solution(mesh):
    placed = (
        P(("group", "dp"), "mp", None, None),
        P(("group", "dp"), "mp", None),
        P(("group", "dp"), "mp", None),
        P(("group", "dp"), "mp"),
        P(("group", "dp")),
        P(("group", "mp"), "dp", None),
    )
    return jax.shard_map(
        functools.partial(body, mesh.shape["dp"], mesh.shape["mp"]),
        mesh=mesh, in_specs=placed, out_specs=P(("group", "mp"), "dp", None), check_vma=False
    )
```

time: 58.9 us -> 41.3 us (0.70)
  local copies, waits for them, and re-layouts: 13.2 us -> 2.83 us
  other arithmetic: 6.95 us -> 0.89 us
  Pallas kernels: 37.9 us -> 36.7 us
    another operation x2 -> x0, local copies, waits for them, and re-layouts: 8.25 us -> none  [body(): blocks = values[0, 0].reshape(slots, BS, BS)]
    concatenate x3 -> x0, other arithmetic: 6.06 us -> none  [the longest x1 5.86 us: body(): jnp.concatenate([blocks, blocks], axis=2)]
    pallas_call x1, Pallas kernels: 37.9 us -> 36.7 us  [body(): pl.pallas_call(functools.partial(kernel, n_dp, n_mp, n_data, n_cells, slo...]
    unnamed x6 -> x7, local copies, waits for them, and re-layouts: 3.95 us -> 2.83 us
    dynamic_slice x1 -> x0, local copies, waits for them, and re-layouts: 0.76 us -> none  [body(): lax.dynamic_slice_in_dim(weights, lax.axis_index('mp') * (owned * BS), ow...]
where the time goes in v2:
time: 41.3 us; the launch traced here: 41.1 us
  Pallas kernels  36.7 us (89%)
  local copies, waits for them, and re-layouts  2.83 us (7%)
  other arithmetic  0.89 us (2%)
  between operations  0.7 us (2%)
    pallas_call x1, Pallas kernels, body(): pl.pallas_call(functools.partial(kernel, n_dp, n_mp, n_data, n_cells, slo...  36.7 us
    unnamed x7, local copies, waits for them, and re-layouts  2.83 us

profile of v2, /device:TPU:0, one launch (start us, length us, event | category | flops | bytes accessed | tf_op | source)
XLA Modules:
  0.0 41.1 jit_solution(4201631403420112550)
XLA Ops:
  0.0 0.0 copy-start.2
  0.7 0.7 %compare_select_fusion = s32[128]{0:T(128)S(1)} fusion(s32[1,1,128]{2,1,0:T(1,128)} %param.8, s32[1,1,128]{2,1,0:T(1,128)} %param.7, s32[]{:T(128)} %bitcast.5), kind=kLoop, calls=%fused_computation.2 | loop fusion | flops 512 | bytes 1540 | tf_op jit(solution)/shard_map/jit(_where)/select_n | solution.py:202
  1.3 0.2 select_reduce_fusion.table
  1.6 0.0 copy-done.2
  1.6 0.0 copy-start
  1.6 1.2 %copy-done = bf16[1,1,128,4096]{3,2,1,0:T(8,128)(2,1)S(1)} copy-done((bf16[1,1,128,4096]{3,2,1,0:T(8,128)(2,1)S(1)}, bf16[1,1,128,4096]{3,2,1,0:T(8,128)(2,1)}, u32[]{:S(2)}) %copy-start) | copy-done | bytes 1048600
  2.8 0.0 copy-start.1
  2.8 0.9 %copy-done.1 = bf16[32,16,64]{2,1,0:T(8,128)(2,1)S(1)} copy-done((bf16[32,16,64]{2,1,0:T(8,128)(2,1)S(1)}, bf16[32,16,64]{2,1,0:T(8,128)(2,1)}, u32[]{:S(2)}) %copy-start.1) | copy-done | bytes 65560
  3.7 36.7 %shard_map.64 = f32[32,16,64]{2,1,0:T(8,128)S(1)} custom-call(s32[1024]{0:T(1024)S(1)} %select_reduce_fusion.table, bf16[128,4096]{1,0:T(8,128)(2,1)S(1)} %bitcast.6, bf16[32,16,64]{2,1,0:T(8,128)(2,1)S(1)} %copy-done.1, f32[1,2048]{1,0:T(1,128)S(1)} %bitcast.7), custom_call_target="tpu_custom_call" | custom-call | tf_op jit(solution)/shard_map/pallas_call | solution.py:209
  40.4 0.7 %copy.9 = f32[32,16,64]{2,1,0:T(8,128)} copy(f32[32,16,64]{2,1,0:T(8,128)S(1)} %shard_map.64) | data formatting | bytes 262144
Async XLA Ops:
  0.0 1.6 %copy-start.2 = (f32[2048]{0:T(1024)S(1)}, f32[2048]{0:T(1024)}, u32[]{:S(2)}) copy-start(f32[2048]{0:T(1024)} %param.10) | copy-start | bytes 24580
  1.6 1.2 %copy-start = (bf16[1,1,128,4096]{3,2,1,0:T(8,128)(2,1)S(1)}, bf16[1,1,128,4096]{3,2,1,0:T(8,128)(2,1)}, u32[]{:S(2)}) copy-start(bf16[1,1,128,4096]{3,2,1,0:T(8,128)(2,1)} %param.6) | copy-start | bytes 3145732
  2.8 0.9 %copy-start.1 = (bf16[32,16,64]{2,1,0:T(8,128)(2,1)S(1)}, bf16[32,16,64]{2,1,0:T(8,128)(2,1)}, u32[]{:S(2)}) copy-start(bf16[32,16,64]{2,1,0:T(8,128)(2,1)} %probes.1) | copy-start | bytes 196612

commit v3 on v2

--- a/solution.py
+++ b/solution.py
@@ -8,6 +8,9 @@
 from jax.sharding import PartitionSpec as P
 
 BS = 64
+STEPS = 32000.0
+TINY = 1e-30
+PITCH = 40
 MESH = pl.DeviceIdType.MESH
 BF16 = jnp.bfloat16
 F32 = jnp.float32
@@ -19,10 +22,10 @@
 
 
 def kernel(n_dp, n_mp, n_data, n_cells, slots,
-           table, values, probes, weights, out,
-           flat, plain, turned, packed, gathered, wide_f32, wide, strips, psend, precv, own_pred,
+           table, values_hbm, probes_hbm, weights, out,
+           values, probes, flat, plain, turned, packed, gathered, wide_f32, wide, strips, psend, precv, csend, crecv, own_pred,
            wgather, total_back, ssend, srecv, own_sketch,
-           gs, gr, ps, pr, ws, wr, ss, sr):
+           local, gs, gr, ps, pr, cs, cr, ws, wr, ss, sr):
     dp, mp = lax.axis_index("dp"), lax.axis_index("mp")
     share = BS // n_dp
     owned = n_data // n_mp
@@ -32,12 +35,21 @@
     hb = BS // 2
     side = lax.broadcasted_iota(jnp.int32, (hb, 2 * BS), 1) < BS
 
+    probes_in = pltpu.make_async_copy(probes_hbm, probes, local.at[0])
+    values_in = pltpu.make_async_copy(values_hbm, values, local.at[1])
+    probes_in.start()
+    values_in.start()
+
     barrier = pltpu.get_barrier_semaphore()
     for off in range(1, n_dp):
         pl.semaphore_signal(barrier, inc=1, device_id={"dp": lax.rem(dp + off, n_dp)}, device_id_type=MESH)
     for off in range(1, n_mp):
         pl.semaphore_signal(barrier, inc=1, device_id={"mp": lax.rem(mp + off, n_mp)}, device_id_type=MESH)
 
+    def partner(x):
+        return sum(lax.rem(mp // (1 << b) + (x >> b) % 2, 2) * (1 << b) for b in range(n_mp.bit_length() - 1))
+
+    probes_in.wait()
     for c in range(half_cells):
         flat[c * share:(c + 1) * share] = jnp.concatenate([probes[c], probes[half_cells + c]], axis=1).astype(F32)
     packed[...] = flat[0:half_cells * share].astype(BF16)
@@ -52,14 +64,15 @@
         remote(packed, gathered.at[off - 1], gs.at[off - 1], gr.at[off - 1],
                "dp", lax.rem(dp + off, n_dp)).start()
 
+    values_in.wait()
     for q in range(hb):
-        flat[pl.ds(q, slots, stride=hb), :] = values[:, q * 2 * BS:(q + 1) * 2 * BS].astype(F32)
+        flat[pl.ds(q, slots, stride=PITCH), :] = values[:, q * 2 * BS:(q + 1) * 2 * BS].astype(F32)
 
     def turn(s, carry):
-        start = pl.multiple_of(s * (8 * hb), 8 * hb)
-        rows = flat[pl.ds(start, 8 * hb), :]
-        plain[pl.ds(s * 8, 8)] = rows.astype(BF16).reshape(8, hb, 2 * BS)
-        turned[pl.ds(s * 8, 8)] = pltpu.roll(rows, BS, 1).astype(BF16).reshape(8, hb, 2 * BS)
+        for t in range(8):
+            rows = flat[pl.ds(pl.multiple_of(s * (8 * PITCH) + t * PITCH, 8), hb), :]
+            plain[s * 8 + t] = rows.astype(BF16)
+            turned[s * 8 + t] = pltpu.roll(rows, BS, 1).astype(BF16)
         return carry
 
     lax.fori_loop(0, slots // 8, turn, 0)
@@ -76,7 +89,11 @@
             strips[pl.ds(base + hb, hb), lanes] = jnp.where(side, turned[a], plain[b])
         return carry
 
-    lax.fori_loop(0, n_data, build, 0)
+    def build_for(k):
+        lax.fori_loop(0, owned, lambda b, carry: build(k * owned + b, carry), 0)
+
+    peers = list(range(n_mp - 1, 0, -1))
+    build_for(partner(peers[0]))
 
     def place(source, d):
         rows = source.astype(F32)
@@ -102,10 +119,16 @@
         full = jnp.dot(strips[rows_of(peer), :], wide[...], preferred_element_type=F32)
         return jnp.where(half, full[:pairs * BS], full[pairs * BS:])
 
-    for off in range(1, n_mp):
-        peer = lax.rem(mp + off, n_mp)
-        psend[off - 1] = predict(peer)
-        remote(psend.at[off - 1], precv.at[off - 1], ps.at[off - 1], pr.at[off - 1], "mp", peer).start()
+    for x in peers:
+        if x != peers[0]:
+            build_for(partner(x))
+        pred = predict(partner(x))
+        top = jnp.maximum(jnp.max(jnp.abs(pred), axis=0, keepdims=True), TINY)
+        psend[x - 1] = jnp.round(pred * (STEPS / top)).astype(jnp.int32).astype(jnp.int16)
+        csend[x - 1] = jnp.broadcast_to(top * (1.0 / STEPS), (8, 2 * BS))
+        remote(csend.at[x - 1], crecv.at[x - 1], cs.at[x - 1], cr.at[x - 1], "mp", partner(x)).start()
+        remote(psend.at[x - 1], precv.at[x - 1], ps.at[x - 1], pr.at[x - 1], "mp", partner(x)).start()
+    build_for(mp)
     own_pred[...] = predict(mp)
 
     i0 = lax.broadcasted_iota(jnp.int32, (2 * BS, 2 * BS), 0)
@@ -122,13 +145,13 @@
          jnp.broadcast_to(sorted_w[0:1, pairs * BS:], (BS, pairs * BS))], axis=0)
 
     total = own_pred[...]
-    for off in range(1, n_mp):
-        remote(psend.at[off - 1], precv.at[off - 1], ps.at[off - 1], pr.at[off - 1], "mp", mp).wait_recv()
-        total = total + precv[off - 1]
+    for x in reversed(peers):
+        remote(csend.at[x - 1], crecv.at[x - 1], cs.at[x - 1], cr.at[x - 1], "mp", mp).wait_recv()
+        remote(psend.at[x - 1], precv.at[x - 1], ps.at[x - 1], pr.at[x - 1], "mp", mp).wait_recv()
+        total = total + precv[x - 1].astype(jnp.int32).astype(F32) * crecv[x - 1, 0:1]
     wgather[0] = (factor * total.T).astype(BF16)
-    for off in range(1, n_mp):
-        remote(wgather.at[0], wgather.at[off], ws.at[off - 1], wr.at[off - 1],
-               "mp", lax.rem(mp + off, n_mp)).start()
+    for x in peers:
+        remote(wgather.at[0], wgather.at[x], ws.at[x - 1], wr.at[x - 1], "mp", partner(x)).start()
 
     group = 8
     gp = group // 2
@@ -146,7 +169,7 @@
             remote(wgather.at[0], wgather.at[off], ws.at[off - 1], wr.at[off - 1], "mp", mp).wait_recv()
         for g in range(n_groups):
             lanes = slice(g * cols, (g + 1) * cols)
-            part = part_of(off, lax.rem(mp + n_mp - off, n_mp), g)
+            part = part_of(off, partner(off) if off else mp, g)
             if off:
                 part = part + total_back[:, lanes]
             if off < n_mp - 1:
@@ -184,6 +207,7 @@
                    ss.at[off - 1, g], sr.at[off - 1, g], "dp", dp).wait_send()
     for off in range(1, n_mp):
         remote(psend.at[off - 1], precv.at[off - 1], ps.at[off - 1], pr.at[off - 1], "mp", mp).wait_send()
+        remote(csend.at[off - 1], crecv.at[off - 1], cs.at[off - 1], cr.at[off - 1], "mp", mp).wait_send()
         remote(wgather.at[0], wgather.at[off], ws.at[off - 1], wr.at[off - 1], "mp", mp).wait_send()
 
 
@@ -209,10 +233,12 @@
     return pl.pallas_call(
         functools.partial(kernel, n_dp, n_mp, n_data, n_cells, slots),
         out_shape=jax.ShapeDtypeStruct((n_cells, share, BS), F32),
-        in_specs=[pl.BlockSpec(memory_space=pltpu.SMEM)] + [vmem] * 3,
+        in_specs=[pl.BlockSpec(memory_space=pltpu.SMEM)] + [pl.BlockSpec(memory_space=pltpu.HBM)] * 2 + [vmem],
         out_specs=vmem,
         scratch_shapes=[
-            pltpu.VMEM((slots * BS // 2, 2 * BS), F32),
+            pltpu.VMEM((slots, BS * BS), BF16),
+            pltpu.VMEM((n_cells, share, BS), BF16),
+            pltpu.VMEM((slots * PITCH, 2 * BS), F32),
             pltpu.VMEM((slots + 1, BS // 2, 2 * BS), BF16),
             pltpu.VMEM((slots + 1, BS // 2, 2 * BS), BF16),
             pltpu.VMEM((half_cells * share, 2 * BS), BF16),
@@ -220,15 +246,19 @@
             pltpu.VMEM((half_cells, BS, 2 * BS), F32),
             pltpu.VMEM((n_cells * BS, 2 * BS), BF16),
             pltpu.VMEM((n_data * BS, n_cells * BS), BF16),
-            pltpu.VMEM((n_mp - 1, pairs * BS, 2 * BS), F32),
-            pltpu.VMEM((n_mp - 1, pairs * BS, 2 * BS), F32),
+            pltpu.VMEM((n_mp - 1, pairs * BS, 2 * BS), jnp.int16),
+            pltpu.VMEM((n_mp - 1, pairs * BS, 2 * BS), jnp.int16),
+            pltpu.VMEM((n_mp - 1, 8, 2 * BS), F32),
+            pltpu.VMEM((n_mp - 1, 8, 2 * BS), F32),
             pltpu.VMEM((pairs * BS, 2 * BS), F32),
             pltpu.VMEM((n_mp, 2 * BS, pairs * BS), BF16),
             pltpu.VMEM((BS, n_cells * BS), F32),
             pltpu.VMEM((n_dp, groups * srows, 2 * BS), BF16),
             pltpu.VMEM((n_dp - 1, groups * srows, 2 * BS), BF16),
             pltpu.VMEM((groups * srows, 2 * BS), F32),
+            dma((2,)),
             dma((n_dp - 1,)), dma((n_dp - 1,)),
+            dma((n_mp - 1,)), dma((n_mp - 1,)),
             dma((n_mp - 1,)), dma((n_mp - 1,)),
             dma((n_mp - 1,)), dma((n_mp - 1,)),
             dma((n_dp - 1, groups)), dma((n_dp - 1, groups)),

time: 41.3 us -> 36.9 us (0.89)
  Pallas kernels: 36.7 us -> 32.3 us
    pallas_call x1, Pallas kernels: 36.7 us -> 32.3 us  [body(): pl.pallas_call(functools.partial(kernel, n_dp, n_mp, n_data, n_cells, slo...]
where the time goes in v3:
time: 36.9 us; the launch traced here: 36.7 us
  Pallas kernels  32.3 us (88%)
  local copies, waits for them, and re-layouts  2.83 us (8%)
  other arithmetic  0.89 us (2%)
  between operations  0.7 us (2%)
    pallas_call x1, Pallas kernels, body(): pl.pallas_call(functools.partial(kernel, n_dp, n_mp, n_data, n_cells, slo...  32.3 us
    unnamed x7, local copies, waits for them, and re-layouts  2.83 us

profile of v3, /device:TPU:0, one launch (start us, length us, event | category | flops | bytes accessed | tf_op | source)
XLA Modules:
  0.0 36.7 jit_solution(5865192975470755450)
XLA Ops:
  0.0 0.0 copy-start.2
  0.7 0.7 %compare_select_fusion = s32[128]{0:T(128)S(1)} fusion(s32[1,1,128]{2,1,0:T(1,128)} %param.8, s32[1,1,128]{2,1,0:T(1,128)} %param.7, s32[]{:T(128)} %bitcast.5), kind=kLoop, calls=%fused_computation.2 | loop fusion | flops 512 | bytes 1540 | tf_op jit(solution)/shard_map/jit(_where)/select_n | solution.py:226
  1.3 0.2 select_reduce_fusion.table
  1.6 0.0 copy-done.2
  1.6 0.0 copy-start
  1.6 1.2 %copy-done = bf16[1,1,128,4096]{3,2,1,0:T(8,128)(2,1)S(1)} copy-done((bf16[1,1,128,4096]{3,2,1,0:T(8,128)(2,1)S(1)}, bf16[1,1,128,4096]{3,2,1,0:T(8,128)(2,1)}, u32[]{:S(2)}) %copy-start) | copy-done | bytes 1048600
  2.8 0.0 copy-start.1
  2.8 0.9 %copy-done.1 = bf16[32,16,64]{2,1,0:T(8,128)(2,1)S(1)} copy-done((bf16[32,16,64]{2,1,0:T(8,128)(2,1)S(1)}, bf16[32,16,64]{2,1,0:T(8,128)(2,1)}, u32[]{:S(2)}) %copy-start.1) | copy-done | bytes 65560
  3.7 32.3 %shard_map.64 = f32[32,16,64]{2,1,0:T(8,128)S(1)} custom-call(s32[1024]{0:T(1024)S(1)} %select_reduce_fusion.table, bf16[128,4096]{1,0:T(8,128)(2,1)S(1)} %bitcast.6, bf16[32,16,64]{2,1,0:T(8,128)(2,1)S(1)} %copy-done.1, f32[1,2048]{1,0:T(1,128)S(1)} %bitcast.7), custom_call_target="tpu_custom_call" | custom-call | tf_op jit(solution)/shard_map/pallas_call | solution.py:233
  36.0 0.7 %copy.9 = f32[32,16,64]{2,1,0:T(8,128)} copy(f32[32,16,64]{2,1,0:T(8,128)S(1)} %shard_map.64) | data formatting | bytes 262144
Async XLA Ops:
  0.0 1.6 %copy-start.2 = (f32[2048]{0:T(1024)S(1)}, f32[2048]{0:T(1024)}, u32[]{:S(2)}) copy-start(f32[2048]{0:T(1024)} %param.10) | copy-start | bytes 24580
  1.6 1.2 %copy-start = (bf16[1,1,128,4096]{3,2,1,0:T(8,128)(2,1)S(1)}, bf16[1,1,128,4096]{3,2,1,0:T(8,128)(2,1)}, u32[]{:S(2)}) copy-start(bf16[1,1,128,4096]{3,2,1,0:T(8,128)(2,1)} %param.6) | copy-start | bytes 3145732
  2.8 0.9 %copy-start.1 = (bf16[32,16,64]{2,1,0:T(8,128)(2,1)S(1)}, bf16[32,16,64]{2,1,0:T(8,128)(2,1)}, u32[]{:S(2)}) copy-start(bf16[32,16,64]{2,1,0:T(8,128)(2,1)} %probes_hbm.1) | copy-start | bytes 196612

commit v4 on v3

--- a/solution.py
+++ b/solution.py
@@ -89,11 +89,8 @@
             strips[pl.ds(base + hb, hb), lanes] = jnp.where(side, turned[a], plain[b])
         return carry
 
-    def build_for(k):
-        lax.fori_loop(0, owned, lambda b, carry: build(k * owned + b, carry), 0)
-
+    lax.fori_loop(0, n_data, build, 0)
     peers = list(range(n_mp - 1, 0, -1))
-    build_for(partner(peers[0]))
 
     def place(source, d):
         rows = source.astype(F32)
@@ -120,15 +117,12 @@
         return jnp.where(half, full[:pairs * BS], full[pairs * BS:])
 
     for x in peers:
-        if x != peers[0]:
-            build_for(partner(x))
         pred = predict(partner(x))
         top = jnp.maximum(jnp.max(jnp.abs(pred), axis=0, keepdims=True), TINY)
         psend[x - 1] = jnp.round(pred * (STEPS / top)).astype(jnp.int32).astype(jnp.int16)
         csend[x - 1] = jnp.broadcast_to(top * (1.0 / STEPS), (8, 2 * BS))
         remote(csend.at[x - 1], crecv.at[x - 1], cs.at[x - 1], cr.at[x - 1], "mp", partner(x)).start()
         remote(psend.at[x - 1], precv.at[x - 1], ps.at[x - 1], pr.at[x - 1], "mp", partner(x)).start()
-    build_for(mp)
     own_pred[...] = predict(mp)
 
     i0 = lax.broadcasted_iota(jnp.int32, (2 * BS, 2 * BS), 0)
@@ -180,17 +174,16 @@
                 piece = jnp.concatenate(
                     [both[p * BS + d * share:p * BS + (d + 1) * share] for p in range(gp)], axis=0)
                 ssend[d, g * rows:(g + 1) * rows] = piece.astype(BF16)
-
-                @pl.when(dp == d)
-                def _():
-                    own_sketch[g * rows:(g + 1) * rows] = piece
+            own_sketch[g * gp * BS:(g + 1) * gp * BS] = both
             for o in range(1, n_dp):
                 peer = lax.rem(dp + o, n_dp)
                 remote(ssend.at[peer, pl.ds(g * rows, rows)], srecv.at[o - 1, pl.ds(g * rows, rows)],
                        ss.at[o - 1, g], sr.at[o - 1, g], "dp", peer).start()
 
     for g in range(n_groups):
-        acc = own_sketch[g * rows:(g + 1) * rows]
+        acc = jnp.concatenate(
+            [own_sketch[pl.ds((g * gp + p) * BS + pl.multiple_of(dp * share, share), share), :] for p in range(gp)],
+            axis=0)
         for off in range(1, n_dp):
             remote(ssend.at[0, pl.ds(g * rows, rows)], srecv.at[off - 1, pl.ds(g * rows, rows)],
                    ss.at[off - 1, g], sr.at[off - 1, g], "dp", dp).wait_recv()
@@ -255,7 +248,7 @@
             pltpu.VMEM((BS, n_cells * BS), F32),
             pltpu.VMEM((n_dp, groups * srows, 2 * BS), BF16),
             pltpu.VMEM((n_dp - 1, groups * srows, 2 * BS), BF16),
-            pltpu.VMEM((groups * srows, 2 * BS), F32),
+            pltpu.VMEM((half_cells * BS, 2 * BS), F32),
             dma((2,)),
             dma((n_dp - 1,)), dma((n_dp - 1,)),
             dma((n_mp - 1,)), dma((n_mp - 1,)),
@@ -264,7 +257,7 @@
             dma((n_dp - 1, groups)), dma((n_dp - 1, groups)),
         ],
         compiler_params=pltpu.CompilerParams(
-            collective_id=0, has_side_effects=True, vmem_limit_bytes=48 * 1024 * 1024),
+            collective_id=0, has_side_effects=True, vmem_limit_bytes=60 * 1024 * 1024),
     )(table, values[0, 0], probes, weights.reshape(1, -1))
 
 

time: 36.9 us -> 36 us (0.976)
  local copies, waits for them, and re-layouts: 2.83 us -> 2.33 us
  Pallas kernels: 32.3 us -> 31.9 us
    select_n x1, other arithmetic: 0.68 us -> 0.01 us  [body(): where = jnp.where(live, rows[0, 0] * n_cells + cols[0, 0], -1)]
    reduce_min x1, other arithmetic: 0.21 us -> 0.81 us  [body(): jnp.min(jnp.where(hit, jnp.arange(slots, dtype=jnp.int32)[None, :], slots...]
    unnamed x7 -> x5, local copies, waits for them, and re-layouts: 2.83 us -> 2.33 us
    pallas_call x1, Pallas kernels: 32.3 us -> 31.9 us  [body(): pl.pallas_call(functools.partial(kernel, n_dp, n_mp, n_data, n_cells, slo...]
where the time goes in v4:
time: 36 us; the launch traced here: 35.7 us
  Pallas kernels  31.9 us (89%)
  local copies, waits for them, and re-layouts  2.33 us (6%)
  other arithmetic  0.81 us (2%)
  between operations  0.68 us (2%)
    pallas_call x1, Pallas kernels, body(): pl.pallas_call(functools.partial(kernel, n_dp, n_mp, n_data, n_cells, slo...  31.9 us
    unnamed x5, local copies, waits for them, and re-layouts  2.33 us
    reduce_min x1, other arithmetic, body(): jnp.min(jnp.where(hit, jnp.arange(slots, dtype=jnp.int32)[None, :], slots...  0.81 us

profile of v4, /device:TPU:0, one launch (start us, length us, event | category | flops | bytes accessed | tf_op | source)
XLA Modules:
  0.0 35.7 jit_solution(3429227032591105418)
XLA Ops:
  0.7 0.0 copy-start
  0.7 0.0 copy-start.1
  0.7 0.6 %copy-done = s32[1,1,128]{2,1,0:T(1,128)S(1)} copy-done((s32[1,1,128]{2,1,0:T(1,128)S(1)}, s32[1,1,128]{2,1,0:T(1,128)}, u32[]{:S(2)}) %copy-start) | copy-done | bytes 536
  1.3 0.0 copy-done.1
  1.3 0.8 %select_reduce_fusion.table = s32[1024]{0:T(1024)} fusion(s32[128]{0:T(128)S(1)} %compare_select_fusion), kind=kLoop, calls=%fused_computation | loop fusion | flops 392192 | bytes 4608 | tf_op jit(solution)/shard_map/reduce_min | solution.py:222
  2.1 31.9 %shard_map.64 = f32[32,16,64]{2,1,0:T(8,128)} custom-call(s32[1024]{0:T(1024)} %select_reduce_fusion.table, bf16[128,4096]{1,0:T(8,128)(2,1)} %bitcast.6, bf16[32,16,64]{2,1,0:T(8,128)(2,1)} %probes_hbm.1, f32[1,2048]{1,0:T(1,128)} %bitcast.7), custom_call_target="tpu_custom_call" | custom-call | tf_op jit(solution)/shard_map/pallas_call | solution.py:226
  34.0 1.7 %copy.9 = f32[32,16,64]{2,1,0:T(8,128)} copy(f32[32,16,64]{2,1,0:T(8,128)} %shard_map.64) | data formatting | bytes 262144
  (1 shorter events, 0.0 us)
Async XLA Ops:
  0.7 0.7 %copy-start = (s32[1,1,128]{2,1,0:T(1,128)S(1)}, s32[1,1,128]{2,1,0:T(1,128)}, u32[]{:S(2)}) copy-start(s32[1,1,128]{2,1,0:T(1,128)} %param.8) | copy-start | bytes 1540
  0.7 0.7 %copy-start.1 = (s32[1,1,128]{2,1,0:T(1,128)S(1)}, s32[1,1,128]{2,1,0:T(1,128)}, u32[]{:S(2)}) copy-start(s32[1,1,128]{2,1,0:T(1,128)} %param.7) | copy-start | bytes 1540

commit v5 on v4

--- a/solution.py
+++ b/solution.py
@@ -158,7 +158,7 @@
         return jnp.dot(left, strips[rows_of(k), g * cols:(g + 1) * cols], preferred_element_type=F32)
 
     n_groups = n_cells // group
-    for off in range(n_mp):
+    for step, off in enumerate([0] + peers):
         if off:
             remote(wgather.at[0], wgather.at[off], ws.at[off - 1], wr.at[off - 1], "mp", mp).wait_recv()
         for g in range(n_groups):
@@ -166,7 +166,7 @@
             part = part_of(off, partner(off) if off else mp, g)
             if off:
                 part = part + total_back[:, lanes]
-            if off < n_mp - 1:
+            if step < n_mp - 1:
                 total_back[:, lanes] = part
                 continue
             both = jnp.concatenate([part[:, :gp * BS], part[:, gp * BS:]], axis=0).T

time: 36 us -> 36 us (level)
  no operation moved by 1% of the time
where the time goes in v5:
time: 36 us; the launch traced here: 35.7 us
  Pallas kernels  31.9 us (89%)
  local copies, waits for them, and re-layouts  2.33 us (6%)
  other arithmetic  0.81 us (2%)
  between operations  0.68 us (2%)
    pallas_call x1, Pallas kernels, body(): pl.pallas_call(functools.partial(kernel, n_dp, n_mp, n_data, n_cells, slo...  31.9 us
    unnamed x5, local copies, waits for them, and re-layouts  2.33 us
    reduce_min x1, other arithmetic, body(): jnp.min(jnp.where(hit, jnp.arange(slots, dtype=jnp.int32)[None, :], slots...  0.81 us

profile of v5, /device:TPU:0, one launch (start us, length us, event | category | flops | bytes accessed | tf_op | source)
XLA Modules:
  0.0 35.7 jit_solution(326903043409652320)
XLA Ops:
  0.7 0.0 copy-start
  0.7 0.0 copy-start.1
  0.7 0.6 %copy-done = s32[1,1,128]{2,1,0:T(1,128)S(1)} copy-done((s32[1,1,128]{2,1,0:T(1,128)S(1)}, s32[1,1,128]{2,1,0:T(1,128)}, u32[]{:S(2)}) %copy-start) | copy-done | bytes 536
  1.3 0.0 copy-done.1
  1.3 0.8 %select_reduce_fusion.table = s32[1024]{0:T(1024)} fusion(s32[128]{0:T(128)S(1)} %compare_select_fusion), kind=kLoop, calls=%fused_computation | loop fusion | flops 392192 | bytes 4608 | tf_op jit(solution)/shard_map/reduce_min | solution.py:222
  2.1 31.9 %shard_map.64 = f32[32,16,64]{2,1,0:T(8,128)} custom-call(s32[1024]{0:T(1024)} %select_reduce_fusion.table, bf16[128,4096]{1,0:T(8,128)(2,1)} %bitcast.6, bf16[32,16,64]{2,1,0:T(8,128)(2,1)} %probes_hbm.1, f32[1,2048]{1,0:T(1,128)} %bitcast.7), custom_call_target="tpu_custom_call" | custom-call | tf_op jit(solution)/shard_map/pallas_call | solution.py:226
  34.0 1.7 %copy.9 = f32[32,16,64]{2,1,0:T(8,128)} copy(f32[32,16,64]{2,1,0:T(8,128)} %shard_map.64) | data formatting | bytes 262144
  (1 shorter events, 0.0 us)
Async XLA Ops:
  0.7 0.7 %copy-start = (s32[1,1,128]{2,1,0:T(1,128)S(1)}, s32[1,1,128]{2,1,0:T(1,128)}, u32[]{:S(2)}) copy-start(s32[1,1,128]{2,1,0:T(1,128)} %param.8) | copy-start | bytes 1540
  0.7 0.7 %copy-start.1 = (s32[1,1,128]{2,1,0:T(1,128)S(1)}, s32[1,1,128]{2,1,0:T(1,128)}, u32[]{:S(2)}) copy-start(s32[1,1,128]{2,1,0:T(1,128)} %param.7) | copy-start | bytes 1540
